TPU v7x, 256 devices: a whole 4x4x8 slice. The times are simulated.
256 devices in a mesh: dp: 32 (over z_hi, x, core), sect: 8 (over y, z_lo).
Axes of the slice: x: 4, y: 4, z: 8 (z_hi: 4, z_lo: 2; z = z_hi * 2 + z_lo), core: 2. Of those that a mesh axis runs over, the one named last changes fastest.
Arguments:
- latent: bfloat16 [32, 2, 32, 256, 128], P('dp', None, 'sect'), may hold values from -6 to 6
- target: bfloat16 [32, 2, 32, 256, 128], P('dp', None, 'sect'), may hold values from -6 to 6
- w_dec: bfloat16 [2, 3, 3, 128, 128], replicated, may hold values from -0.125 to 0.125
- w_disc: bfloat16 [3, 3, 128, 128], replicated, may hold values from -0.1875 to 0.1875
- w_head: float32 [128], replicated, may hold values from -4 to 4
- w_perc: bfloat16 [128, 128], replicated, may hold values from -0.5 to 0.5
Outputs:
- grad_dec: float32 [2, 3, 3, 128, 128], replicated
All inputs are finite; a program needn't handle non-finite values.
Results may differ from a plain program's by a relative error of at most 0.00065.
Values may be sent and summed in bfloat16 or wider, within the bound.
A program may use at most 64 MiB of HBM per device.

v0:
```python
import functools

import jax
import jax.numpy as jnp
from jax import lax
from jax.experimental import pallas as pl
from jax.experimental.pallas import tpu as pltpu
from jax.sharding import PartitionSpec as P

MESH = pl.DeviceIdType.MESH
F32 = jnp.float32
BF16 = jnp.bfloat16
FRAMES, ROWS, COLS, CH = 2, 4, 256, 128
NX, NY, NZ = 4, 4, 8
TAPS = 18
HALF = TAPS * CH // 2
PARTS = 3
PART = HALF // PARTS
PIECE = PART // (NX * NY)
PLANE = sorted(range(1, NX * NY), key=lambda d: -min(d // NY, NX - d // NY) - min(d % NY, NY - d % NY))
LINE = sorted(range(1, NZ), key=lambda d: -min(d, NZ - d))


def slope(value):
    sig = jax.nn.sigmoid(value)
    return sig * (1.0 + value * (1.0 - sig))


def shifted(tile):
    at = lax.broadcasted_iota(jnp.int32, tile.shape, 0)
    before = jnp.where(at == 0, 0.0, pltpu.roll(tile, 1, 0))
    after = jnp.where(at == COLS - 1, 0.0, pltpu.roll(tile, COLS - 1, 0))
    return before.astype(BF16), tile.astype(BF16), after.astype(BF16)


def dot(a, b):
    return jnp.dot(a, b, preferred_element_type=F32)


def kernel(
    lat_hbm, tgt_hbm, wdec_hbm, wdisc_hbm, whead_hbm, wperc_hbm,
    out_ref,
    xs, x3, xt, tgt, wa, wx, wd, wb, wp, wq, wdv, whead_ref, wperc_ref, rec, rhalo, r3, g3, feat, slp, p3,
    buf, cin, red, r1, r2,
    lsem, hsend, hrecv, near, tsem, sent, crecv, v1, v2, v3, v4,
):
    dp, sect = lax.axis_index("dp"), lax.axis_index("sect")
    core, px = lax.rem(dp, 2), lax.rem(dp // 2, NX)
    py, pz = sect // 2, (dp // 8) * 2 + lax.rem(sect, 2)

    def at(x, y, z, c):
        return ((z // 2) * 8 + x * 2 + c, y * 2 + lax.rem(z, 2))

    other = at(px, py, pz, 1 - core)

    def plane(d):
        return at(lax.rem(px + d // NY, NX), lax.rem(py + d % NY, NY), pz, core)

    def line(d):
        return at(px, py, lax.rem(pz + d, NZ), core)

    low = lax.rem(pz, 2)
    home = low == core
    block = 2 * py + core
    has_up, has_down = block > 0, block < 2 * NY - 1
    partner = at(px, py, pz + 1 - 2 * low, 1 - core)
    up = at(px, py - (1 - core), pz, 1 - core)
    down = at(px, py + core, pz, 1 - core)

    bar = pltpu.get_barrier_semaphore()

    def greet(who):
        pl.semaphore_signal(bar, inc=1, device_id=who, device_id_type=MESH)

    @pl.when(has_up)
    def _():
        greet(up)

    @pl.when(has_down)
    def _():
        greet(down)

    greet(partner)
    greet(other)
    for d in range(1, NX * NY):
        greet(plane(d))
    for d in range(1, NZ):
        greet(line(d))

    loads = [
        pltpu.make_async_copy(wdec_hbm.at[1], wa.at[:, pl.ds(0, CH)], lsem.at[0]),
        pltpu.make_async_copy(wdec_hbm.at[0], wa.at[:, pl.ds(CH, CH)], lsem.at[1]),
        pltpu.make_async_copy(wdisc_hbm, wdv, lsem.at[2]),
        pltpu.make_async_copy(wperc_hbm, wperc_ref, lsem.at[3]),
        pltpu.make_async_copy(whead_hbm, whead_ref, lsem.at[4]),
    ]
    for cp in loads:
        cp.start()

    zrow = jnp.zeros((FRAMES, COLS, CH), BF16)

    @pl.when(jnp.logical_not(has_up))
    def _():
        xs[:, 0] = zrow
        xs[:, 1] = zrow
        rhalo[0] = zrow

    @pl.when(jnp.logical_not(has_down))
    def _():
        xs[:, 6] = zrow
        xs[:, 7] = zrow
        rhalo[1] = zrow

    def widen(dst, t, idx, tile):
        for j, piece in enumerate(shifted(tile)):
            dst[t, idx, :, j * CH:(j + 1) * CH] = piece

    def widen_x(row):
        for t in range(FRAMES):
            tile = xs[t, row + 2]
            widen(x3, t, row + 2, tile.astype(F32))
            if -1 <= row <= ROWS:
                xt[t, row + 1] = tile.T

    def around(src, t, idx):
        return jnp.concatenate([src[t, idx - 1], src[t, idx], src[t, idx + 1]], axis=1)

    def four(src, t, idx):
        return jnp.concatenate([src[t, idx + q] for q in range(4)], axis=1)

    def pre_rows(r):
        first = dot(jnp.concatenate([around(x3, 0, r + 2 + n) for n in range(2)], axis=0), wa[...])
        second = dot(four(x3, 1, r + 1), wx[...])
        for n in range(2):
            row, span = r + n, slice(n * COLS, (n + 1) * COLS)
            for t in range(FRAMES):
                pre = first[span, :CH] if t == 0 else first[span, CH:] + second[:, n * CH:(n + 1) * CH]
                sig = jax.nn.sigmoid(pre)
                value = pre * sig
                if row < 0:
                    value = jnp.where(has_up, value, 0.0)
                elif row >= ROWS:
                    value = jnp.where(has_down, value, 0.0)
                else:
                    slp[t, row] = sig * (1.0 + pre * (1.0 - sig))
                widen(r3, t, row + 2, value)
                if row in (1, 2):
                    rec[2 - row, t] = value.astype(BF16)

    def disc_rows(r):
        res = dot(jnp.concatenate([four(r3, t, r + 1) for t in range(FRAMES)], axis=0), wd[...])
        for n in range(2):
            row = r + n
            for t in range(FRAMES):
                grad = -whead_ref[...] * slope(res[t * COLS:(t + 1) * COLS, n * CH:(n + 1) * CH])
                if row < 0:
                    grad = jnp.where(has_up, grad, 0.0)
                elif row >= ROWS:
                    grad = jnp.where(has_down, grad, 0.0)
                widen(g3, t, row + 1, grad)

    def feat_rows():
        lhs = [
            jnp.concatenate([r3[t, r + 2 + n, :, CH:2 * CH] for n in range(2)], axis=1)
            for r in (0, 2) for t in range(FRAMES)
        ]
        feat[...] = dot(jnp.concatenate(lhs, axis=0), wp[...])

    def back_rows(r):
        return dot(jnp.concatenate([four(g3, t, r) for t in range(FRAMES)], axis=0), wb[...])

    def grad_rows(r, back):
        miss = []
        for t in range(FRAMES):
            at_row = (r + t) * COLS
            goal = jnp.concatenate([tgt[t, r + n].astype(F32) for n in range(2)], axis=1)
            miss.append((feat[at_row:at_row + COLS] - goal).astype(BF16))
        res = back + dot(jnp.concatenate(miss, axis=0), wq[...])
        for n in range(2):
            for t in range(FRAMES):
                grad = res[t * COLS:(t + 1) * COLS, n * CH:(n + 1) * CH] * slp[t, r + n]
                for j, piece in enumerate(shifted(grad)):
                    lane = (t * 3 + 2 - j) * CH
                    p3[(r + n) * COLS:(r + n + 1) * COLS, lane:lane + CH] = piece

    def weight_rows():
        def left(t):
            return jnp.concatenate([xt[t, r:r + 3].reshape(3 * CH, COLS) for r in range(ROWS)], axis=1)

        both = dot(left(0), p3[...])
        late = dot(left(1), p3[:, 3 * CH:])
        for k in range(2):
            for i in range(3):
                for j in range(3):
                    rows, lanes = slice(i * CH, (i + 1) * CH), slice(j * CH, (j + 1) * CH)
                    span = pl.ds(((k * 3 + i) * 3 + j) * CH, CH)
                    if k:
                        buf[span] = both[rows, lanes] + late[rows, lanes]
                    else:
                        buf[span] = both[rows, (3 + j) * CH:(4 + j) * CH]

    def remote(src, dst, send, recv, who):
        cp = pltpu.make_async_remote_copy(
            src_ref=src, dst_ref=dst, send_sem=send, recv_sem=recv,
            device_id=who, device_id_type=MESH,
        )
        cp.start()

    def settle(like, sem):
        pltpu.make_async_copy(like, like, sem).wait()

    ROW, FOUR = xs.at[:, 0], xs.at[:, pl.ds(0, ROWS)]

    @pl.when(home)
    def _():
        for row in range(ROWS):
            pltpu.make_async_copy(lat_hbm.at[:, row], xs.at[:, row + 2], hrecv.at[row]).start()
        pltpu.make_async_copy(tgt_hbm, tgt, tsem).start()

    pl.semaphore_wait(bar, NX * NY - 1 + NZ - 1 + 2 + has_up.astype(jnp.int32) + has_down.astype(jnp.int32))

    def order(c, k):
        return k + c * (ROWS - 1 - 2 * k)

    @pl.when(jnp.logical_not(home))
    def _():
        for k in range(ROWS):
            row = order(1 - core, k)
            remote(lat_hbm.at[:, row], xs.at[:, row + 2], hsend.at[0], hrecv.at[row], partner)
        remote(tgt_hbm, tgt, hsend.at[1], tsem, partner)

    for n in (2, 3, 4):
        loads[n].wait()

    def band(dst, tap):
        dst[...] = jnp.zeros_like(dst)
        for n in range(2):
            for i in range(3):
                for j in range(3):
                    row = ((i + n) * 3 + j) * CH
                    dst[row:row + CH, n * CH:(n + 1) * CH] = tap(i * 3 + j)

    band(wd, lambda k: wdv[k * CH:(k + 1) * CH])
    band(wb, lambda k: wdv[(8 - k) * CH:(9 - k) * CH].T)
    loads[0].wait()
    band(wx, lambda k: wa[k * CH:(k + 1) * CH, :CH])
    loads[1].wait()
    wp[...] = jnp.zeros_like(wp)
    wq[...] = jnp.zeros_like(wq)
    for n in range(2):
        span = slice(n * CH, (n + 1) * CH)
        wp[span, span] = wperc_ref[...]
        wq[span, span] = wperc_ref[...].T

    def pass_on(row):
        settle(ROW, hrecv.at[row])
        if row <= 1:
            @pl.when(has_up)
            def _():
                remote(xs.at[:, row + 2], xs.at[:, row + 6], hsend.at[2], near.at[2 + row], up)
        else:
            @pl.when(has_down)
            def _():
                remote(xs.at[:, row + 2], xs.at[:, row - 2], hsend.at[3], near.at[3 - row], down)
        widen_x(row)

    @pl.when(core == 0)
    def _():
        for row in range(ROWS):
            pass_on(row)

    @pl.when(core == 1)
    def _():
        for row in reversed(range(ROWS)):
            pass_on(row)

    pre_rows(1)

    @pl.when(has_up)
    def _():
        remote(rec.at[1], rhalo.at[1], hsend.at[2], near.at[5], up)

    @pl.when(has_down)
    def _():
        remote(rec.at[0], rhalo.at[0], hsend.at[3], near.at[4], down)

    def arrived(step):
        @pl.when(has_up)
        def _():
            settle(ROW, near.at[(0, 1, 4)[step]])

        @pl.when(has_down)
        def _():
            settle(ROW, near.at[(2, 3, 5)[step]])

    arrived(0)
    widen_x(-1)
    widen_x(ROWS)
    arrived(1)
    widen_x(-2)
    widen_x(ROWS + 1)
    pre_rows(-1)
    pre_rows(ROWS - 1)
    feat_rows()
    disc_rows(1)

    arrived(2)
    for side, row in ((0, -2), (1, ROWS + 1)):
        for t in range(FRAMES):
            widen(r3, t, row + 2, rhalo[side, t].astype(F32))
    disc_rows(-1)
    disc_rows(ROWS - 1)
    back = [back_rows(r) for r in (0, 2)]
    settle(FOUR, tsem)
    for n in range(2):
        grad_rows(2 * n, back[n])
    weight_rows()

    mine, theirs = core * HALF, (1 - core) * HALF
    spot = px * NY + py
    for g in range(PARTS):
        remote(
            buf.at[pl.ds(pl.multiple_of(theirs + g * PART, 8), PART)],
            cin.at[pl.ds(g * PART, PART)], sent.at[0], crecv.at[g], other,
        )

    def piece(g, q):
        return pl.ds(pl.multiple_of(g * PART + q * PIECE, 8), PIECE)

    def whole(g, q):
        return pl.ds(pl.multiple_of(mine + g * PART + q * PIECE, 8), PIECE)

    for g in range(PARTS):
        part = pl.ds(g * PART, PART)
        settle(cin.at[part], crecv.at[g])
        red[part] = buf[pl.ds(pl.multiple_of(mine + g * PART, 8), PART)] + cin[part]
        for d in PLANE:
            q = lax.rem(px + d // NY, NX) * NY + lax.rem(py + d % NY, NY)
            remote(red.at[piece(g, q)], r1.at[g, spot], sent.at[1], v1.at[g], plane(d))
        r1[g, spot] = red[piece(g, spot)]
    for g in range(PARTS):
        settle(r1.at[g, pl.ds(0, len(PLANE))], v1.at[g])
        total = r1[g, 0]
        for n in range(1, NX * NY):
            total = total + r1[g, n]
        r2[g, pz] = total
        for d in LINE:
            remote(r2.at[g, pz], r2.at[g, pz], sent.at[2], v2.at[g], line(d))
    for g in range(PARTS):
        settle(r2.at[g, pl.ds(0, len(LINE))], v2.at[g])
        total = r2[g, 0]
        for n in range(1, NZ):
            total = total + r2[g, n]
        own = whole(g, spot)
        out_ref[own] = total
        for d in PLANE:
            remote(out_ref.at[own], out_ref.at[own], sent.at[3], v3.at[g], plane(d))
    for g in range(PARTS):
        settle(r1.at[g, pl.ds(0, len(PLANE))], v3.at[g])
        rows = pl.ds(pl.multiple_of(mine + g * PART, 8), PART)
        remote(out_ref.at[rows], out_ref.at[rows], sent.at[4], v4, other)
    settle(cin, v4)

    @pl.when(jnp.logical_not(home))
    def _():
        settle(FOUR, hsend.at[0])
        settle(FOUR, hsend.at[1])

    @pl.when(has_up)
    def _():
        settle(xs.at[:, pl.ds(0, 3)], hsend.at[2])

    @pl.when(has_down)
    def _():
        settle(xs.at[:, pl.ds(0, 3)], hsend.at[3])

    settle(cin, sent.at[0])
    settle(red.at[pl.ds(0, PARTS * len(PLANE) * PIECE)], sent.at[1])
    settle(red.at[pl.ds(0, PARTS * len(LINE) * PIECE)], sent.at[2])
    settle(red.at[pl.ds(0, PARTS * len(PLANE) * PIECE)], sent.at[3])
    settle(cin, sent.at[4])


def per_device(latent, target, w_dec, w_disc, w_head, w_perc):
    hbm = pl.BlockSpec(memory_space=pltpu.HBM)
    vmem = pl.BlockSpec(memory_space=pltpu.VMEM)
    dma = pltpu.SemaphoreType.DMA
    plane, line = NX * NY, NZ
    total = pl.pallas_call(
        kernel,
        out_shape=jax.ShapeDtypeStruct((TAPS * CH, CH), F32),
        in_specs=[hbm] * 6,
        out_specs=vmem,
        scratch_shapes=[
            pltpu.VMEM((FRAMES, ROWS + 4, COLS, CH), BF16),
            pltpu.VMEM((FRAMES, ROWS + 4, COLS, 3 * CH), BF16),
            pltpu.VMEM((FRAMES, ROWS + 2, CH, COLS), BF16),
            pltpu.VMEM((FRAMES, ROWS, COLS, CH), BF16),
            pltpu.VMEM((9 * CH, 2 * CH), BF16),
            pltpu.VMEM((12 * CH, 2 * CH), BF16),
            pltpu.VMEM((12 * CH, 2 * CH), BF16),
            pltpu.VMEM((12 * CH, 2 * CH), BF16),
            pltpu.VMEM((2 * CH, 2 * CH), BF16),
            pltpu.VMEM((2 * CH, 2 * CH), BF16),
            pltpu.VMEM((9 * CH, CH), BF16),
            pltpu.VMEM((1, CH), F32),
            pltpu.VMEM((CH, CH), BF16),
            pltpu.VMEM((2, FRAMES, COLS, CH), BF16),
            pltpu.VMEM((2, FRAMES, COLS, CH), BF16),
            pltpu.VMEM((FRAMES, ROWS + 4, COLS, 3 * CH), BF16),
            pltpu.VMEM((FRAMES, ROWS + 2, COLS, 3 * CH), BF16),
            pltpu.VMEM((FRAMES * ROWS * COLS // 2, 2 * CH), F32),
            pltpu.VMEM((FRAMES, ROWS, COLS, CH), F32),
            pltpu.VMEM((ROWS * COLS, FRAMES * 3 * CH), BF16),
            pltpu.VMEM((TAPS * CH, CH), F32),
            pltpu.VMEM((HALF, CH), F32),
            pltpu.VMEM((HALF, CH), F32),
            pltpu.VMEM((PARTS, plane, PIECE, CH), F32),
            pltpu.VMEM((PARTS, line, PIECE, CH), F32),
            dma((5,)), dma((4,)), dma((ROWS,)), dma((6,)), dma, dma((5,)), dma((PARTS,)),
            dma((PARTS,)), dma((PARTS,)), dma((PARTS,)), dma,
        ],
        compiler_params=pltpu.CompilerParams(
            collective_id=0, has_side_effects=True, vmem_limit_bytes=48 << 20
        ),
        name="tokenizer_step",
    )(
        *(pltpu.with_memory_space_constraint(x, pltpu.HBM) for x in (
            latent[0], target[0], w_dec.reshape(2, 9 * CH, CH), w_disc.reshape(9 * CH, CH),
            w_head.reshape(1, CH), w_perc,
        ))
    )
    pixels = lax.axis_size("dp") * FRAMES * ROWS * lax.axis_size("sect") * COLS
    total = total / jnp.sqrt(jnp.float32(pixels))
    return total.reshape(2, 3, 3, CH, CH)


def solution(mesh):
    in_specs = (
        P("dp", None, "sect", None, None),
        P("dp", None, "sect", None, None),
        P(),
        P(),
        P(),
        P(),
    )
    return jax.shard_map(
        per_device, mesh=mesh, in_specs=in_specs, out_specs=P(), check_vma=False
    )
```

profile of v0, /device:TPU:1, one launch (start us, length us, event | category | flops | bytes accessed | tf_op | source)
XLA Modules:
  0.0 51.0 jit_solution(7593943897632972469)
XLA Ops:
  0.0 49.9 %tokenizer_step.1 = f32[2304,128]{1,0:T(8,128)S(1)} custom-call(bf16[2,4,256,128]{3,2,1,0:T(8,128)(2,1)} %bitcast.7, bf16[2,4,256,128]{3,2,1,0:T(8,128)(2,1)} %bitcast.8, bf16[2,1152,128]{2,1,0:T(8,128)(2,1)} %bitcast.6, bf16[1152,128]{1,0:T(8,128)(2,1)} %bitcast.9, f32[1,128]{1,0:T(1,128)} %bitcast.10, bf16[128,128]{1,0:T(8,128)(2,1)} %wperc_hbm.1), custom_call_target="tpu_custom_call" | custom-call | tf_op jit(solution)/shard_map/tokenizer_step/pallas_call | solution.py:389
  49.9 1.1 %broadcast_multiply_fusion = f32[2304,128]{1,0:T(8,128)} fusion(f32[2304,128]{1,0:T(8,128)S(1)} %tokenizer_step.1), kind=kLoop, calls=%fused_computation | loop fusion | flops 294912 | bytes 2359296 | tf_op jit(solution)/shard_map/div | solution.py:434
where the time goes:
time: 51.1 us; the launch traced here: 51 us
  Pallas kernels  49.9 us (98%)
  other arithmetic  1.12 us (2%)
    pallas_call x1, Pallas kernels, per_device(): pl.pallas_call(kernel, out_shape=jax.ShapeDtypeStruct((TAPS * CH, CH), F3...  49.9 us
    div x1, other arithmetic, per_device(): total = total / jnp.sqrt(jnp.float32(pixels))  1.12 us

commit v1 on v0

--- a/solution.py
+++ b/solution.py
@@ -14,7 +14,8 @@
 NX, NY, NZ = 4, 4, 8
 TAPS = 18
 HALF = TAPS * CH // 2
-PARTS = 3
+PARTS = 9
+LINED = [0, 3, 6]
 PART = HALF // PARTS
 PIECE = PART // (NX * NY)
 PLANE = sorted(range(1, NX * NY), key=lambda d: -min(d // NY, NX - d // NY) - min(d % NY, NY - d % NY))
@@ -41,7 +42,7 @@
     lat_hbm, tgt_hbm, wdec_hbm, wdisc_hbm, whead_hbm, wperc_hbm,
     out_ref,
     xs, x3, xt, tgt, wa, wx, wd, wb, wp, wq, wdv, whead_ref, wperc_ref, rec, rhalo, r3, g3, feat, slp, p3,
-    buf, cin, red, r1, r2,
+    buf, cin, red, r1, r2, l1, l2,
     lsem, hsend, hrecv, near, tsem, sent, crecv, v1, v2, v3, v4,
 ):
     dp, sect = lax.axis_index("dp"), lax.axis_index("sect")
@@ -317,46 +318,66 @@
     weight_rows()
 
     mine, theirs = core * HALF, (1 - core) * HALF
-    spot = px * NY + py
     for g in range(PARTS):
         remote(
             buf.at[pl.ds(pl.multiple_of(theirs + g * PART, 8), PART)],
             cin.at[pl.ds(g * PART, PART)], sent.at[0], crecv.at[g], other,
         )
 
-    def piece(g, q):
-        return pl.ds(pl.multiple_of(g * PART + q * PIECE, 8), PIECE)
-
-    def whole(g, q):
-        return pl.ds(pl.multiple_of(mine + g * PART + q * PIECE, 8), PIECE)
+    def rows_at(base, g, q, size):
+        return pl.ds(pl.multiple_of(base + g * PART + q * size, 8), size)
+
+    def in_plane(d):
+        return lax.rem(px + d // NY, NX) * NY + lax.rem(py + d % NY, NY)
+
+    def in_line(d):
+        return lax.rem(pz + d, NZ)
+
+    class Plane:
+        steps, place, who, spot = PLANE, in_plane, plane, px * NY + py
+
+    class Line:
+        steps, place, who, spot = LINE, in_line, line, pz
+
+    def route(g):
+        if g in LINED:
+            return Line, Plane, l1.at[LINED.index(g)], l2.at[LINED.index(g)]
+        return Plane, Line, r1.at[g], r2.at[g]
+
+    def add_up(slots):
+        total = slots[0]
+        for n in range(1, slots.shape[0]):
+            total = total + slots[n]
+        return total
 
     for g in range(PARTS):
+        first, _, land, _ = route(g)
+        size = land.shape[1]
         part = pl.ds(g * PART, PART)
         settle(cin.at[part], crecv.at[g])
         red[part] = buf[pl.ds(pl.multiple_of(mine + g * PART, 8), PART)] + cin[part]
-        for d in PLANE:
-            q = lax.rem(px + d // NY, NX) * NY + lax.rem(py + d % NY, NY)
-            remote(red.at[piece(g, q)], r1.at[g, spot], sent.at[1], v1.at[g], plane(d))
-        r1[g, spot] = red[piece(g, spot)]
+        for d in first.steps:
+            remote(
+                red.at[rows_at(0, g, first.place(d), size)], land.at[first.spot],
+                sent.at[1], v1.at[g], first.who(d),
+            )
+        land[first.spot] = red[rows_at(0, g, first.spot, size)]
     for g in range(PARTS):
-        settle(r1.at[g, pl.ds(0, len(PLANE))], v1.at[g])
-        total = r1[g, 0]
-        for n in range(1, NX * NY):
-            total = total + r1[g, n]
-        r2[g, pz] = total
-        for d in LINE:
-            remote(r2.at[g, pz], r2.at[g, pz], sent.at[2], v2.at[g], line(d))
+        first, second, land, meet = route(g)
+        settle(land.at[pl.ds(0, len(first.steps))], v1.at[g])
+        meet[second.spot] = add_up(land)
+        for d in second.steps:
+            remote(meet.at[second.spot], meet.at[second.spot], sent.at[2], v2.at[g], second.who(d))
     for g in range(PARTS):
-        settle(r2.at[g, pl.ds(0, len(LINE))], v2.at[g])
-        total = r2[g, 0]
-        for n in range(1, NZ):
-            total = total + r2[g, n]
-        own = whole(g, spot)
-        out_ref[own] = total
-        for d in PLANE:
-            remote(out_ref.at[own], out_ref.at[own], sent.at[3], v3.at[g], plane(d))
+        first, second, land, meet = route(g)
+        settle(meet.at[pl.ds(0, len(second.steps))], v2.at[g])
+        own = rows_at(mine, g, first.spot, land.shape[1])
+        out_ref[own] = add_up(meet)
+        for d in first.steps:
+            remote(out_ref.at[own], out_ref.at[own], sent.at[3], v3.at[g], first.who(d))
     for g in range(PARTS):
-        settle(r1.at[g, pl.ds(0, len(PLANE))], v3.at[g])
+        first, _, land, _ = route(g)
+        settle(land.at[pl.ds(0, len(first.steps))], v3.at[g])
         rows = pl.ds(pl.multiple_of(mine + g * PART, 8), PART)
         remote(out_ref.at[rows], out_ref.at[rows], sent.at[4], v4, other)
     settle(cin, v4)
@@ -375,9 +396,11 @@
         settle(xs.at[:, pl.ds(0, 3)], hsend.at[3])
 
     settle(cin, sent.at[0])
-    settle(red.at[pl.ds(0, PARTS * len(PLANE) * PIECE)], sent.at[1])
-    settle(red.at[pl.ds(0, PARTS * len(LINE) * PIECE)], sent.at[2])
-    settle(red.at[pl.ds(0, PARTS * len(PLANE) * PIECE)], sent.at[3])
+    outer = (PARTS - len(LINED)) * len(PLANE) * PIECE + len(LINED) * len(LINE) * PART // NZ
+    inner = (PARTS - len(LINED)) * len(LINE) * PIECE + len(LINED) * len(PLANE) * PART // NZ
+    settle(buf.at[pl.ds(0, outer)], sent.at[1])
+    settle(buf.at[pl.ds(0, inner)], sent.at[2])
+    settle(buf.at[pl.ds(0, outer)], sent.at[3])
     settle(cin, sent.at[4])
 
 
@@ -417,6 +440,8 @@
             pltpu.VMEM((HALF, CH), F32),
             pltpu.VMEM((PARTS, plane, PIECE, CH), F32),
             pltpu.VMEM((PARTS, line, PIECE, CH), F32),
+            pltpu.VMEM((len(LINED), line, PART // NZ, CH), F32),
+            pltpu.VMEM((len(LINED), plane, PART // NZ, CH), F32),
             dma((5,)), dma((4,)), dma((ROWS,)), dma((6,)), dma, dma((5,)), dma((PARTS,)),
             dma((PARTS,)), dma((PARTS,)), dma((PARTS,)), dma,
         ],

time: 51.1 us -> 48.8 us (0.955)
  Pallas kernels: 49.9 us -> 47.6 us
    pallas_call x1, Pallas kernels: 49.9 us -> 47.6 us  [per_device(): pl.pallas_call(kernel, out_shape=jax.ShapeDtypeStruct((TAPS * CH, CH), F3...]
where the time goes in v1:
time: 48.8 us; the launch traced here: 48.7 us
  Pallas kernels  47.6 us (98%)
  other arithmetic  1.12 us (2%)
    pallas_call x1, Pallas kernels, per_device(): pl.pallas_call(kernel, out_shape=jax.ShapeDtypeStruct((TAPS * CH, CH), F3...  47.6 us
    div x1, other arithmetic, per_device(): total = total / jnp.sqrt(jnp.float32(pixels))  1.12 us

profile of v1, /device:TPU:1, one launch (start us, length us, event | category | flops | bytes accessed | tf_op | source)
XLA Modules:
  0.0 48.7 jit_solution(12777677757272729824)
XLA Ops:
  0.0 47.6 %tokenizer_step.1 = f32[2304,128]{1,0:T(8,128)S(1)} custom-call(bf16[2,4,256,128]{3,2,1,0:T(8,128)(2,1)} %bitcast.7, bf16[2,4,256,128]{3,2,1,0:T(8,128)(2,1)} %bitcast.8, bf16[2,1152,128]{2,1,0:T(8,128)(2,1)} %bitcast.6, bf16[1152,128]{1,0:T(8,128)(2,1)} %bitcast.9, f32[1,128]{1,0:T(1,128)} %bitcast.10, bf16[128,128]{1,0:T(8,128)(2,1)} %wperc_hbm.1), custom_call_target="tpu_custom_call" | custom-call | tf_op jit(solution)/shard_map/tokenizer_step/pallas_call | solution.py:412
  47.6 1.1 %broadcast_multiply_fusion = f32[2304,128]{1,0:T(8,128)} fusion(f32[2304,128]{1,0:T(8,128)S(1)} %tokenizer_step.1), kind=kLoop, calls=%fused_computation | loop fusion | flops 294912 | bytes 2359296 | tf_op jit(solution)/shard_map/div | solution.py:459

commit v2 on v1

--- a/solution.py
+++ b/solution.py
@@ -73,6 +73,8 @@
     def greet(who):
         pl.semaphore_signal(bar, inc=1, device_id=who, device_id_type=MESH)
 
+    greet(partner)
+
     @pl.when(has_up)
     def _():
         greet(up)
@@ -81,7 +83,6 @@
     def _():
         greet(down)
 
-    greet(partner)
     greet(other)
     for d in range(1, NX * NY):
         greet(plane(d))
@@ -218,18 +219,6 @@
             pltpu.make_async_copy(lat_hbm.at[:, row], xs.at[:, row + 2], hrecv.at[row]).start()
         pltpu.make_async_copy(tgt_hbm, tgt, tsem).start()
 
-    pl.semaphore_wait(bar, NX * NY - 1 + NZ - 1 + 2 + has_up.astype(jnp.int32) + has_down.astype(jnp.int32))
-
-    def order(c, k):
-        return k + c * (ROWS - 1 - 2 * k)
-
-    @pl.when(jnp.logical_not(home))
-    def _():
-        for k in range(ROWS):
-            row = order(1 - core, k)
-            remote(lat_hbm.at[:, row], xs.at[:, row + 2], hsend.at[0], hrecv.at[row], partner)
-        remote(tgt_hbm, tgt, hsend.at[1], tsem, partner)
-
     for n in (2, 3, 4):
         loads[n].wait()
 
@@ -253,6 +242,18 @@
         wp[span, span] = wperc_ref[...]
         wq[span, span] = wperc_ref[...].T
 
+    pl.semaphore_wait(bar, NX * NY - 1 + NZ - 1 + 2 + has_up.astype(jnp.int32) + has_down.astype(jnp.int32))
+
+    def order(c, k):
+        return k + c * (ROWS - 1 - 2 * k)
+
+    @pl.when(jnp.logical_not(home))
+    def _():
+        for k in range(ROWS):
+            row = order(1 - core, k)
+            remote(lat_hbm.at[:, row], xs.at[:, row + 2], hsend.at[0], hrecv.at[row], partner)
+        remote(tgt_hbm, tgt, hsend.at[1], tsem, partner)
+
     def pass_on(row):
         settle(ROW, hrecv.at[row])
         if row <= 1:
@@ -344,6 +345,13 @@
             return Line, Plane, l1.at[LINED.index(g)], l2.at[LINED.index(g)]
         return Plane, Line, r1.at[g], r2.at[g]
 
+    def turned(group, g):
+        if g % 2 == 0:
+            return group.steps
+        if group is Line:
+            return [NZ - d for d in group.steps]
+        return [(NX - d // NY) % NX * NY + (NY - d % NY) % NY for d in group.steps]
+
     def add_up(slots):
         total = slots[0]
         for n in range(1, slots.shape[0]):
@@ -356,7 +364,7 @@
         part = pl.ds(g * PART, PART)
         settle(cin.at[part], crecv.at[g])
         red[part] = buf[pl.ds(pl.multiple_of(mine + g * PART, 8), PART)] + cin[part]
-        for d in first.steps:
+        for d in turned(first, g):
             remote(
                 red.at[rows_at(0, g, first.place(d), size)], land.at[first.spot],
                 sent.at[1], v1.at[g], first.who(d),
@@ -366,14 +374,14 @@
         first, second, land, meet = route(g)
         settle(land.at[pl.ds(0, len(first.steps))], v1.at[g])
         meet[second.spot] = add_up(land)
-        for d in second.steps:
+        for d in turned(second, g):
             remote(meet.at[second.spot], meet.at[second.spot], sent.at[2], v2.at[g], second.who(d))
     for g in range(PARTS):
         first, second, land, meet = route(g)
         settle(meet.at[pl.ds(0, len(second.steps))], v2.at[g])
         own = rows_at(mine, g, first.spot, land.shape[1])
         out_ref[own] = add_up(meet)
-        for d in first.steps:
+        for d in turned(first, g):
             remote(out_ref.at[own], out_ref.at[own], sent.at[3], v3.at[g], first.who(d))
     for g in range(PARTS):
         first, _, land, _ = route(g)

time: 48.8 us -> 48.9 us (level)
  no operation moved by 1% of the time
where the time goes in v2:
time: 48.9 us; the launch traced here: 48.8 us
  Pallas kernels  47.7 us (98%)
  other arithmetic  1.12 us (2%)
    pallas_call x1, Pallas kernels, per_device(): pl.pallas_call(kernel, out_shape=jax.ShapeDtypeStruct((TAPS * CH, CH), F3...  47.7 us
    div x1, other arithmetic, per_device(): total = total / jnp.sqrt(jnp.float32(pixels))  1.12 us

profile of v2, /device:TPU:1, one launch (start us, length us, event | category | flops | bytes accessed | tf_op | source)
XLA Modules:
  0.0 48.8 jit_solution(16202605513280629664)
XLA Ops:
  0.0 47.7 %tokenizer_step.1 = f32[2304,128]{1,0:T(8,128)S(1)} custom-call(bf16[2,4,256,128]{3,2,1,0:T(8,128)(2,1)} %bitcast.7, bf16[2,4,256,128]{3,2,1,0:T(8,128)(2,1)} %bitcast.8, bf16[2,1152,128]{2,1,0:T(8,128)(2,1)} %bitcast.6, bf16[1152,128]{1,0:T(8,128)(2,1)} %bitcast.9, f32[1,128]{1,0:T(1,128)} %bitcast.10, bf16[128,128]{1,0:T(8,128)(2,1)} %wperc_hbm.1), custom_call_target="tpu_custom_call" | custom-call | tf_op jit(solution)/shard_map/tokenizer_step/pallas_call | solution.py:420
  47.7 1.1 %broadcast_multiply_fusion = f32[2304,128]{1,0:T(8,128)} fusion(f32[2304,128]{1,0:T(8,128)S(1)} %tokenizer_step.1), kind=kLoop, calls=%fused_computation | loop fusion | flops 294912 | bytes 2359296 | tf_op jit(solution)/shard_map/div | solution.py:467

commit v3 on v1

--- a/solution.py
+++ b/solution.py
@@ -14,10 +14,13 @@
 NX, NY, NZ = 4, 4, 8
 TAPS = 18
 HALF = TAPS * CH // 2
-PARTS = 9
-LINED = [0, 3, 6]
-PART = HALF // PARTS
-PIECE = PART // (NX * NY)
+LINED = [0, 2, 4]
+PLANED = [1, 3, 5]
+SIZES = [128, 256, 128, 256, 128, 256]
+PARTS = len(SIZES)
+STARTS = [sum(SIZES[:g]) for g in range(PARTS)]
+PIECE = SIZES[PLANED[0]] // (NX * NY)
+STRIP = SIZES[LINED[0]] // NZ
 PLANE = sorted(range(1, NX * NY), key=lambda d: -min(d // NY, NX - d // NY) - min(d % NY, NY - d % NY))
 LINE = sorted(range(1, NZ), key=lambda d: -min(d, NZ - d))
 
@@ -320,12 +323,12 @@
     mine, theirs = core * HALF, (1 - core) * HALF
     for g in range(PARTS):
         remote(
-            buf.at[pl.ds(pl.multiple_of(theirs + g * PART, 8), PART)],
-            cin.at[pl.ds(g * PART, PART)], sent.at[0], crecv.at[g], other,
+            buf.at[pl.ds(pl.multiple_of(theirs + STARTS[g], 8), SIZES[g])],
+            cin.at[pl.ds(STARTS[g], SIZES[g])], sent.at[0], crecv.at[g], other,
         )
 
     def rows_at(base, g, q, size):
-        return pl.ds(pl.multiple_of(base + g * PART + q * size, 8), size)
+        return pl.ds(pl.multiple_of(base + STARTS[g] + q * size, 8), size)
 
     def in_plane(d):
         return lax.rem(px + d // NY, NX) * NY + lax.rem(py + d % NY, NY)
@@ -342,7 +345,14 @@
     def route(g):
         if g in LINED:
             return Line, Plane, l1.at[LINED.index(g)], l2.at[LINED.index(g)]
-        return Plane, Line, r1.at[g], r2.at[g]
+        return Plane, Line, r1.at[PLANED.index(g)], r2.at[PLANED.index(g)]
+
+    def turned(group, g):
+        if g % 2 == 0:
+            return group.steps
+        if group is Line:
+            return [NZ - d for d in group.steps]
+        return [(NX - d // NY) % NX * NY + (NY - d % NY) % NY for d in group.steps]
 
     def add_up(slots):
         total = slots[0]
@@ -353,10 +363,10 @@
     for g in range(PARTS):
         first, _, land, _ = route(g)
         size = land.shape[1]
-        part = pl.ds(g * PART, PART)
+        part = pl.ds(STARTS[g], SIZES[g])
         settle(cin.at[part], crecv.at[g])
-        red[part] = buf[pl.ds(pl.multiple_of(mine + g * PART, 8), PART)] + cin[part]
-        for d in first.steps:
+        red[part] = buf[pl.ds(pl.multiple_of(mine + STARTS[g], 8), SIZES[g])] + cin[part]
+        for d in turned(first, g):
             remote(
                 red.at[rows_at(0, g, first.place(d), size)], land.at[first.spot],
                 sent.at[1], v1.at[g], first.who(d),
@@ -366,19 +376,19 @@
         first, second, land, meet = route(g)
         settle(land.at[pl.ds(0, len(first.steps))], v1.at[g])
         meet[second.spot] = add_up(land)
-        for d in second.steps:
+        for d in turned(second, g):
             remote(meet.at[second.spot], meet.at[second.spot], sent.at[2], v2.at[g], second.who(d))
     for g in range(PARTS):
         first, second, land, meet = route(g)
         settle(meet.at[pl.ds(0, len(second.steps))], v2.at[g])
         own = rows_at(mine, g, first.spot, land.shape[1])
         out_ref[own] = add_up(meet)
-        for d in first.steps:
+        for d in turned(first, g):
             remote(out_ref.at[own], out_ref.at[own], sent.at[3], v3.at[g], first.who(d))
     for g in range(PARTS):
         first, _, land, _ = route(g)
         settle(land.at[pl.ds(0, len(first.steps))], v3.at[g])
-        rows = pl.ds(pl.multiple_of(mine + g * PART, 8), PART)
+        rows = pl.ds(pl.multiple_of(mine + STARTS[g], 8), SIZES[g])
         remote(out_ref.at[rows], out_ref.at[rows], sent.at[4], v4, other)
     settle(cin, v4)
 
@@ -396,8 +406,8 @@
         settle(xs.at[:, pl.ds(0, 3)], hsend.at[3])
 
     settle(cin, sent.at[0])
-    outer = (PARTS - len(LINED)) * len(PLANE) * PIECE + len(LINED) * len(LINE) * PART // NZ
-    inner = (PARTS - len(LINED)) * len(LINE) * PIECE + len(LINED) * len(PLANE) * PART // NZ
+    outer = (PARTS - len(LINED)) * len(PLANE) * PIECE + len(LINED) * len(LINE) * STRIP
+    inner = (PARTS - len(LINED)) * len(LINE) * PIECE + len(LINED) * len(PLANE) * STRIP
     settle(buf.at[pl.ds(0, outer)], sent.at[1])
     settle(buf.at[pl.ds(0, inner)], sent.at[2])
     settle(buf.at[pl.ds(0, outer)], sent.at[3])
@@ -438,10 +448,10 @@
             pltpu.VMEM((TAPS * CH, CH), F32),
             pltpu.VMEM((HALF, CH), F32),
             pltpu.VMEM((HALF, CH), F32),
-            pltpu.VMEM((PARTS, plane, PIECE, CH), F32),
-            pltpu.VMEM((PARTS, line, PIECE, CH), F32),
-            pltpu.VMEM((len(LINED), line, PART // NZ, CH), F32),
-            pltpu.VMEM((len(LINED), plane, PART // NZ, CH), F32),
+            pltpu.VMEM((len(PLANED), plane, PIECE, CH), F32),
+            pltpu.VMEM((len(PLANED), line, PIECE, CH), F32),
+            pltpu.VMEM((len(LINED), line, STRIP, CH), F32),
+            pltpu.VMEM((len(LINED), plane, STRIP, CH), F32),
             dma((5,)), dma((4,)), dma((ROWS,)), dma((6,)), dma, dma((5,)), dma((PARTS,)),
             dma((PARTS,)), dma((PARTS,)), dma((PARTS,)), dma,
         ],

time: 48.8 us -> 48.8 us (level)
  no operation moved by 1% of the time
where the time goes in v3:
time: 48.8 us; the launch traced here: 48.7 us
  Pallas kernels  47.6 us (98%)
  other arithmetic  1.12 us (2%)
    pallas_call x1, Pallas kernels, per_device(): pl.pallas_call(kernel, out_shape=jax.ShapeDtypeStruct((TAPS * CH, CH), F3...  47.6 us
    div x1, other arithmetic, per_device(): total = total / jnp.sqrt(jnp.float32(pixels))  1.12 us

profile of v3, /device:TPU:1, one launch (start us, length us, event | category | flops | bytes accessed | tf_op | source)
XLA Modules:
  0.0 48.7 jit_solution(5350941797907125485)
XLA Ops:
  0.0 47.6 %tokenizer_step.1 = f32[2304,128]{1,0:T(8,128)S(1)} custom-call(bf16[2,4,256,128]{3,2,1,0:T(8,128)(2,1)} %bitcast.7, bf16[2,4,256,128]{3,2,1,0:T(8,128)(2,1)} %bitcast.8, bf16[2,1152,128]{2,1,0:T(8,128)(2,1)} %bitcast.6, bf16[1152,128]{1,0:T(8,128)(2,1)} %bitcast.9, f32[1,128]{1,0:T(1,128)} %bitcast.10, bf16[128,128]{1,0:T(8,128)(2,1)} %wperc_hbm.1), custom_call_target="tpu_custom_call" | custom-call | tf_op jit(solution)/shard_map/tokenizer_step/pallas_call | solution.py:422
  47.6 1.1 %broadcast_multiply_fusion = f32[2304,128]{1,0:T(8,128)} fusion(f32[2304,128]{1,0:T(8,128)S(1)} %tokenizer_step.1), kind=kLoop, calls=%fused_computation | loop fusion | flops 294912 | bytes 2359296 | tf_op jit(solution)/shard_map/div | solution.py:469
